TPU v7x, 512 devices: a whole 4x4x16 slice. The times are simulated.
512 devices in a mesh: rep: 32 (over z, x_lo), gz: 16 (over x_hi, y, core).
Axes of the slice: x: 4 (x_hi: 2, x_lo: 2; x = x_hi * 2 + x_lo), y: 4, z: 16, core: 2. Of those that a mesh axis runs over, the one named last changes fastest.
Arguments:
- lattice_field: float32 [192, 64, 4096], P('rep', 'gz'), may hold values from -4 to 4
- langevin_noise: float32 [2, 192, 64, 4096], P(None, 'rep', 'gz'), may hold values from -5 to 5
- masses: float32 [64, 4096], P('gz'), may hold values from -2 to 2
- counts: int32 [192], replicated, may hold values from 0 to 49, as said below
- dest_slots: int32 [192], replicated, may hold values from 0 to 191, each once
- mode_bins: int32 [64, 64, 33], P('gz'), may hold values from 0 to 15, as said below
Outputs:
- resampled: float32 [192, 64, 4096], P('rep', 'gz')
- propagator: float32 [192, 16], P('rep')
Inputs may be any that keep to these rules, and one draw needn't show every extreme that they name: The counts sum to 192; in each aligned block of 6 replicas (those of one index of rep) at most 3 counts are nonzero, and exactly 3 in some block. `dest_slots`: A permutation of the 192 slots. `mode_bins`: the bin depends only on n_y^2 + n_z^2 + kx^2 with n = min(k, 64 - k), and never falls as that grows; every bin holds at least one mode.
All inputs are finite; a program needn't handle non-finite values.
Results may differ from a plain program's by a relative error of at most 0.00007.
Values sent between devices are 32-bit elements; how exact they have to be, the bound alone decides.
No kernel may reach another device: no remote copies, remote signals or barrier semaphores. Data moves between devices by JAX's collectives and lax.ppermute only.
A program may use at most 64 MiB of HBM per device.

v0:
```python
import jax
import jax.numpy as jnp
from jax import lax
from jax.sharding import PartitionSpec as P

L = 64
SWEEPS = 2
NBINS = 16
step_size = 0.1
quartic = 0.5


def with_halo(block, sides, width):
    for axis, dim in sides:
        count = lax.axis_size(axis)
        forward = [(i, i + 1) for i in range(count - 1)]
        forward.append((count - 1, 0))
        backward = [(target, source) for source, target in forward]
        low = lax.ppermute(
            lax.slice_in_dim(block, block.shape[dim] - width, None, axis=dim), axis, forward
        )
        high = lax.ppermute(lax.slice_in_dim(block, 0, width, axis=dim), axis, backward)
        block = jnp.concatenate([low, block, high], axis=dim)
    return block


def in_plane(center):
    grid = center.reshape(center.shape[0], center.shape[1], L, L)
    across = jnp.roll(grid, 1, axis=3) + jnp.roll(grid, -1, axis=3)
    return jnp.roll(center, L, axis=2) + jnp.roll(center, -L, axis=2) + across.reshape(center.shape)


def update(center, below, above, site_masses, noise_now):
    beside = below + above + in_plane(center)
    drift = 6.0 * center - beside + site_masses[None] * center + quartic * center * center * center
    return center - step_size * drift + jnp.sqrt(2.0 * step_size) * noise_now


def angle_tables(rows, columns):
    product = jnp.arange(rows)[:, None] * jnp.arange(columns)[None, :] % L
    theta = 2.0 * jnp.pi / L * product.astype(jnp.float32)
    return (jnp.cos(theta), jnp.sin(theta))


def make_weights(mode_bins):
    half = L // 2 + 1
    ordered = jnp.transpose(mode_bins, (1, 0, 2))
    wave_x = jnp.arange(half)
    weight_x = jnp.where((wave_x == 0) | (wave_x == L // 2), 1.0, 2.0).astype(jnp.float32)
    onehot = (ordered[..., None] == jnp.arange(NBINS)[None, None, None, :]).astype(jnp.float32)
    return (onehot * weight_x[None, None, :, None]).reshape(-1, NBINS)


def transform(slabs, weights):
    half = L // 2 + 1
    exact = lax.Precision.HIGHEST
    cos_half, sin_half = angle_tables(L, half)
    cos_full, sin_full = angle_tables(L, L)
    along_x = jnp.concatenate([cos_half, -sin_half], axis=1)
    count, depth = (slabs.shape[0], slabs.shape[1])
    grid = slabs.reshape(count, depth, L, L)
    first = jnp.einsum("nzyx,xk->nzyk", grid, along_x, precision=exact)
    real_x, imag_x = (first[..., :half], first[..., half:])
    real_y = jnp.einsum("qy,nzyk->nzqk", cos_full, real_x, precision=exact) + jnp.einsum(
        "qy,nzyk->nzqk", sin_full, imag_x, precision=exact
    )
    imag_y = jnp.einsum("qy,nzyk->nzqk", cos_full, imag_x, precision=exact) - jnp.einsum(
        "qy,nzyk->nzqk", sin_full, real_x, precision=exact
    )
    merged = jnp.concatenate([real_y, imag_y], axis=3).reshape(count, depth, L * 2 * half)
    block = lax.all_to_all(merged, "gz", split_axis=2, concat_axis=1, tiled=True)
    items = block.shape[0]
    pencil = block.reshape(items, L, -1, 2 * half)
    real_p = pencil[..., :half]
    imag_p = pencil[..., half:]
    real_z = jnp.einsum("pz,mzqk->mpqk", cos_full, real_p, precision=exact) + jnp.einsum(
        "pz,mzqk->mpqk", sin_full, imag_p, precision=exact
    )
    imag_z = jnp.einsum("pz,mzqk->mpqk", cos_full, imag_p, precision=exact) - jnp.einsum(
        "pz,mzqk->mpqk", sin_full, real_p, precision=exact
    )
    power = real_z * real_z + imag_z * imag_z
    binned = jnp.dot(power.reshape(items, -1), weights, precision=exact)
    binned_total, weight_total = lax.psum((binned, jnp.sum(weights, axis=0)), "gz")
    return binned_total / (float(L**3) * weight_total)


def local(lattice_field, langevin_noise, masses, counts, dest_slots, mode_bins):
    local_count = lattice_field.shape[0]
    weights = make_weights(mode_bins)
    swept = lattice_field
    for turn in range(SWEEPS):
        padded = with_halo(swept, (("gz", 1),), 1)
        swept = update(padded[:, 1:-1], padded[:, :-2], padded[:, 2:], masses, langevin_noise[turn])
    base = lax.axis_index("rep") * local_count
    ends = jnp.cumsum(counts)
    position = jnp.argsort(dest_slots)
    mine_position = lax.dynamic_slice_in_dim(position, base, local_count)
    mine_source = jnp.sum((ends[None, :] <= mine_position[:, None]).astype(jnp.int32), axis=1)
    empty = jnp.zeros_like(swept)
    piece = lax.all_gather(swept, "rep", axis=0, tiled=True)
    found = (mine_source >= 0) & (mine_source < piece.shape[0])
    chosen = jnp.take(piece, jnp.clip(mine_source, 0, piece.shape[0] - 1), axis=0)
    resampled = jnp.where(found[:, None, None], chosen, empty)
    propagator = transform(resampled, weights)
    return (resampled, propagator)


def solution(mesh):
    in_specs = (
        P("rep", "gz", None),
        P(None, "rep", "gz", None),
        P("gz", None),
        P(),
        P(),
        P("gz", None, None),
    )
    out_specs = (P("rep", "gz", None), P("rep", None))
    return jax.shard_map(local, mesh=mesh, in_specs=in_specs, out_specs=out_specs, check_vma=False)
```

profile of v0, /device:TPU:38, one launch (start us, length us, event | category | flops | bytes accessed | tf_op | source)
XLA Modules:
  0.0 452.3 jit_solution(2166895266252879648)
XLA Ops:
  7.2 1.3 fusion.124
  8.5 1.9 collective-permute-start
  10.4 7.3 %collective-permute-start.1 = (f32[6,1,4096]{2,1,0:T(1,128)S(1)}, f32[6,1,4096]{2,1,0:T(1,128)S(1)}, u32[]{:S(2)}, u32[]{:S(2)}) collective-permute-start(f32[6,1,4096]{2,1,0:T(1,128)S(1)} %get-tuple-element.27), channel_id=1, source_target_pairs={{1,0},{2,1},{3,2},{4,3},{5,4},{6,5},{7,6},{8,7},{9,8},{10,9},{11,1... | collective-permute-start | bytes 294920 | tf_op jit(solution)/shard_map/ppermute | solution.py:22
  17.7 1.4 reshape.93
  19.7 0.7 copy-done
  20.7 0.7 fusion.123
  21.3 0.5 maximum_add_fusion
  21.8 0.3 add.129
  22.2 0.6 copy-done.4
  23.0 1.8 fusion.23
  24.7 0.4 reshape.94
  26.0 0.8 fusion.121
  26.9 1.9 collective-permute-start.2
  28.8 7.4 %collective-permute-start.3 = (f32[6,1,4096]{2,1,0:T(1,128)}, f32[6,1,4096]{2,1,0:T(1,128)S(1)}, u32[]{:S(2)}, u32[]{:S(2)}) collective-permute-start(f32[6,1,4096]{2,1,0:T(1,128)} %get-tuple-element.21), channel_id=1, source_target_pairs={{1,0},{2,1},{3,2},{4,3},{5,4},{6,5},{7,6},{8,7},{9,8},{10,9},{11,1... | collective-permute-start | bytes 294920 | tf_op jit(solution)/shard_map/ppermute | solution.py:22
  36.3 0.5 maximum_add_fusion.1
  36.8 0.3 add.138
  37.1 1.5 collective-permute-done.3
  38.6 1.6 fusion.27
  40.4 0.3 reduce-window.9
  41.3 3.2 sort.17
  45.3 281.6 %all-gather.2.cloned.1.call-done = f32[192,4,4096]{2,1,0:T(4,128)} async-done(((f32[6,4,4096]{2,1,0:T(4,128)}), f32[192,4,4096]{2,1,0:T(4,128)}) %all-gather.2.cloned.1.call-update) | async-done | bytes 12582928 | tf_op jit(solution)/shard_map/all_gather | solution.py:101
  326.9 5.4 %gather_fusion = f32[6,4,4096]{2,1,0:T(4,128)S(1)} fusion(f32[192,4,4096]{2,1,0:T(4,128)} %all-gather.2.cloned.1.call-done, s32[1024]{0:T(1024)S(1)} %pad_clamp_fusion), kind=kCustom, calls=%fused_computation | custom fusion | bytes 786456 | tf_op jit(solution)/shard_map/jit(_take)/gather | solution.py:103
  332.3 0.4 gather.7
  332.7 0.8 fusion.7
  333.5 1.4 fusion.14
  335.0 1.6 fusion.10
  336.6 1.6 fusion.5
  338.2 1.4 fusion.4
  339.7 9.3 %copy.65 = f32[6,4,64,66]{0,1,3,2:T(4,128)} copy(f32[6,4,64,66]{2,3,1,0:T(8,128)S(1)} %pad_maximum_fusion) | data formatting | bytes 811008 | tf_op jit(solution)/shard_map/reshape | solution.py:70
  349.0 12.4 %reshape.110 = f32[16,1,6336]{2,1,0:T(1,128)} reshape(f32[4224,4,6]{2,1,0:T(4,128)} %bitcast.64) | data formatting | bytes 811008
  361.4 7.3 %all-to-all-start = ((f32[16,1,6336]{2,1,0:T(1,128)}), f32[16,1,6336]{2,1,0:T(1,128)S(1)}, u32[]{:S(2)}, u32[]{:S(2)}) async-start(f32[16,1,6336]{2,1,0:T(1,128)} %reshape.110), calls=%async_computation | async-start | bytes 819200 | tf_op jit(solution)/shard_map/all_to_all | solution.py:71
  368.7 0.9 select_select_fusion
  369.6 7.4 %all-to-all-done = f32[16,1,6336]{2,1,0:T(1,128)S(1)} async-done(((f32[16,1,6336]{2,1,0:T(1,128)}), f32[16,1,6336]{2,1,0:T(1,128)S(1)}, u32[]{:S(2)}, u32[]{:S(2)}) %all-to-all-start) | async-done | bytes 405536 | tf_op jit(solution)/shard_map/all_to_all | solution.py:71
  376.9 0.5 broadcast.218
  377.5 1.6 reduce.2
  379.1 15.2 %reshape.111 = f32[4224,4,6]{2,1,0:T(4,128)} reshape(f32[16,6336]{1,0:T(8,128)S(1)} %reduce.2) | data formatting | bytes 811008
  394.3 7.6 %copy.51 = f32[6,4,16,264]{3,1,2,0:T(4,128)S(1)} copy(f32[6,4,16,264]{0,1,3,2:T(4,128)} %bitcast.65) | data formatting | bytes 811008 | tf_op jit(solution)/shard_map/all_to_all | solution.py:71
  401.9 0.6 reshape.96
  402.5 0.5 fusion.114
  402.9 0.3 copy.67
  403.3 0.7 fusion.56
  404.0 0.3 copy.68
  404.3 0.7 fusion.54
  405.0 0.7 fusion.3
  405.7 0.7 fusion.2
  406.4 1.6 convolution_bitcast_fusion
  407.9 36.9 %all-reduce.1 = (f32[6,16]{1,0:T(8,128)S(1)}, f32[16]{0:T(128)S(1)}) all-reduce(f32[6,16]{1,0:T(8,128)S(1)} %convolution_bitcast_fusion, f32[16]{0:T(128)S(1)} %select_reduce_fusion), channel_id=1, replica_groups=mesh['rep'=32,'gz'=16] {'gz'}, use_global_device_ids=true, to_apply=%region_4.5 | all-reduce | flops 112 | bytes 896 | tf_op jit(solution)/shard_map/psum | solution.py:84
  444.9 0.6 broadcast_divide_fusion
  (47 shorter events, 3.7 us)
Async XLA Ops:
  7.2 319.8 %all-gather.2.cloned.1.call-start = ((), (), s32[]{:S(2)}) async-start(), calls=%async_computation.1 | async-start | bytes 12976128 | tf_op jit(solution)/shard_map/all_gather | solution.py:101
  8.5 13.6 %collective-permute-start = (f32[6,1,4096]{2,1,0:T(1,128)S(1)}, f32[6,1,4096]{2,1,0:T(1,128)S(1)}, u32[]{:S(2)}, u32[]{:S(2)}) collective-permute-start(f32[6,1,4096]{2,1,0:T(1,128)S(1)} %get-tuple-element.26), channel_id=1, source_target_pairs={{0,1},{1,2},{2,3},{3,4},{4,5},{5,6},{6,7},{7,8},{8,9},{9,10},{10,1... | collective-permute-start | bytes 294920 | tf_op jit(solution)/shard_map/ppermute | solution.py:19
  10.4 11.7 %collective-permute-start.1 = (f32[6,1,4096]{2,1,0:T(1,128)S(1)}, f32[6,1,4096]{2,1,0:T(1,128)S(1)}, u32[]{:S(2)}, u32[]{:S(2)}) collective-permute-start(f32[6,1,4096]{2,1,0:T(1,128)S(1)} %get-tuple-element.27), channel_id=1, source_target_pairs={{1,0},{2,1},{3,2},{4,3},{5,4},{6,5},{7,6},{8,7},{9,8},{10,9},{11,1... | collective-permute-start | bytes 294920 | tf_op jit(solution)/shard_map/ppermute | solution.py:22
  19.4 1.0 copy-start
  21.8 1.1 copy-start.1
  22.2 0.6 copy-start.4
  22.2 0.7 copy-start.5
  26.9 10.2 %collective-permute-start.2 = (f32[6,1,4096]{2,1,0:T(1,128)}, f32[6,1,4096]{2,1,0:T(1,128)S(1)}, u32[]{:S(2)}, u32[]{:S(2)}) collective-permute-start(f32[6,1,4096]{2,1,0:T(1,128)} %get-tuple-element.20), channel_id=1, source_target_pairs={{0,1},{1,2},{2,3},{3,4},{4,5},{5,6},{6,7},{7,8},{8,9},{9,10},{10,1... | collective-permute-start | bytes 294920 | tf_op jit(solution)/shard_map/ppermute | solution.py:19
  28.8 9.8 %collective-permute-start.3 = (f32[6,1,4096]{2,1,0:T(1,128)}, f32[6,1,4096]{2,1,0:T(1,128)S(1)}, u32[]{:S(2)}, u32[]{:S(2)}) collective-permute-start(f32[6,1,4096]{2,1,0:T(1,128)} %get-tuple-element.21), channel_id=1, source_target_pairs={{1,0},{2,1},{3,2},{4,3},{5,4},{6,5},{7,6},{8,7},{9,8},{10,9},{11,1... | collective-permute-start | bytes 294920 | tf_op jit(solution)/shard_map/ppermute | solution.py:22
  36.8 1.9 copy-start.3
  38.6 1.6 copy-start.2
  38.6 1.8 copy-start.6
  40.2 1.1 copy-start.7
  361.4 15.5 %all-to-all-start = ((f32[16,1,6336]{2,1,0:T(1,128)}), f32[16,1,6336]{2,1,0:T(1,128)S(1)}, u32[]{:S(2)}, u32[]{:S(2)}) async-start(f32[16,1,6336]{2,1,0:T(1,128)} %reshape.110), calls=%async_computation | async-start | bytes 819200 | tf_op jit(solution)/shard_map/all_to_all | solution.py:71
Sparse Core Ops, SparseCore 0:
  40.3 286.5 all-gather.1
where the time goes:
time: 453 us; the launch traced here: 452 us
  waiting for transfers between devices  290 us (64%)
  local copies, waits for them, and re-layouts  61.9 us (14%)
  blocking collectives  36.9 us (8%)
  starting transfers between devices  25.8 us (6%)
  between operations  14.4 us (3%)
  other arithmetic  11.6 us (3%)
  matrix products  11.2 us (2%)
    all_gather x1, waiting for transfers between devices, local(): piece = lax.all_gather(swept, 'rep', axis=0, tiled=True)  282 us
    psum x1, blocking collectives, transform(): lax.psum((binned, jnp.sum(weights, axis=0)), 'gz')  36.9 us
    unnamed x20, local copies, waits for them, and re-layouts  29.8 us
    ppermute x2, starting transfers between devices, with_halo(): lax.ppermute(lax.slice_in_dim(block, 0, width, axis=dim), axis, backward)  14.7 us
    reshape x1, local copies, waits for them, and re-layouts, transform(): jnp.concatenate([real_y, imag_y], axis=3)  9.27 us
  transfers between devices with their start and end apart: 6, of which 3 were waited for; matrix products, arithmetic and copies ran while one was open for 2% of the time, Pallas kernels for 0%

commit v1 on v0

--- a/solution.py
+++ b/solution.py
@@ -98,7 +98,9 @@
     mine_position = lax.dynamic_slice_in_dim(position, base, local_count)
     mine_source = jnp.sum((ends[None, :] <= mine_position[:, None]).astype(jnp.int32), axis=1)
     empty = jnp.zeros_like(swept)
-    piece = lax.all_gather(swept, "rep", axis=0, tiled=True)
+    piece = jnp.concatenate(
+        lax.all_to_all(jnp.stack([swept] * lax.axis_size("rep")), "rep", 0, 0), axis=0
+    )
     found = (mine_source >= 0) & (mine_source < piece.shape[0])
     chosen = jnp.take(piece, jnp.clip(mine_source, 0, piece.shape[0] - 1), axis=0)
     resampled = jnp.where(found[:, None, None], chosen, empty)

time: 453 us -> 722 us (1.59)
  the two profiles are of different devices: /device:TPU:38 before, /device:TPU:6 now
where the time goes in v1:
time: 722 us; the launch traced here: 721 us
  waiting for transfers between devices  546 us (76%)
  local copies, waits for them, and re-layouts  69.3 us (10%)
  starting transfers between devices  45 us (6%)
  blocking collectives  36.9 us (5%)
  matrix products  11.2 us (2%)
  other arithmetic  10.9 us (2%)
    all_to_all x1, waiting for transfers between devices, local(): lax.all_to_all(jnp.stack([swept] * lax.axis_size('rep')), 'rep', 0, 0)  538 us
    psum x1, blocking collectives, transform(): lax.psum((binned, jnp.sum(weights, axis=0)), 'gz')  36.9 us
    unnamed x20, local copies, waits for them, and re-layouts  29.8 us
    all_to_all x1, starting transfers between devices, local(): lax.all_to_all(jnp.stack([swept] * lax.axis_size('rep')), 'rep', 0, 0)  16.9 us
    ppermute x2, starting transfers between devices, with_halo(): lax.ppermute(lax.slice_in_dim(block, 0, width, axis=dim), axis, backward)  14.5 us
  transfers between devices with their start and end apart: 6, of which 3 were waited for; matrix products, arithmetic and copies ran while one was open for 1% of the time, Pallas kernels for 0%

profile of v1, /device:TPU:6, one launch (start us, length us, event | category | flops | bytes accessed | tf_op | source)
XLA Modules:
  0.0 720.7 jit_solution(12837699114552143509)
XLA Ops:
  0.6 1.3 fusion.124
  1.9 1.9 collective-permute-start
  3.9 7.3 %collective-permute-start.1 = (f32[6,1,4096]{2,1,0:T(1,128)S(1)}, f32[6,1,4096]{2,1,0:T(1,128)S(1)}, u32[]{:S(2)}, u32[]{:S(2)}) collective-permute-start(f32[6,1,4096]{2,1,0:T(1,128)S(1)} %get-tuple-element.27), channel_id=1, source_target_pairs={{1,0},{2,1},{3,2},{4,3},{5,4},{6,5},{7,6},{8,7},{9,8},{10,9},{11,1... | collective-permute-start | bytes 294920 | tf_op jit(solution)/shard_map/ppermute | solution.py:22
  11.1 1.4 reshape.98
  13.1 0.7 copy-done
  14.1 0.7 fusion.123
  14.8 0.5 maximum_add_fusion
  15.3 0.3 add.129
  15.6 0.6 copy-done.4
  16.4 1.8 fusion.23
  18.1 0.4 reshape.99
  19.4 0.8 fusion.121
  20.3 1.9 collective-permute-start.2
  22.2 7.3 %collective-permute-start.3 = (f32[6,1,4096]{2,1,0:T(1,128)S(1)}, f32[6,1,4096]{2,1,0:T(1,128)S(1)}, u32[]{:S(2)}, u32[]{:S(2)}) collective-permute-start(f32[6,1,4096]{2,1,0:T(1,128)S(1)} %get-tuple-element.21), channel_id=1, source_target_pairs={{1,0},{2,1},{3,2},{4,3},{5,4},{6,5},{7,6},{8,7},{9,8},{10,9},{11,1... | collective-permute-start | bytes 294920 | tf_op jit(solution)/shard_map/ppermute | solution.py:22
  29.5 0.5 maximum_add_fusion.1
  30.0 0.3 add.138
  30.3 1.4 collective-permute-done.3
  31.7 0.8 fusion.27
  32.5 7.6 %stack.2 = f32[32,6,4,4096]{3,2,1,0:T(4,128)} broadcast(f32[6,4,4096]{2,1,0:T(4,128)S(1)} %fusion.27), dimensions={1,2,3} | broadcast | bytes 12976128 | tf_op jit(solution)/shard_map/stack | solution.py:102
  40.1 16.9 %all-to-all-start = ((f32[32,6,4,4096]{3,2,1,0:T(4,128)}), f32[32,6,4,4096]{3,2,1,0:T(4,128)}, u32[]{:S(2)}, u32[]{:S(2)}) async-start(f32[32,6,4,4096]{3,2,1,0:T(4,128)} %stack.2), calls=%async_computation | async-start | bytes 25165824 | tf_op jit(solution)/shard_map/all_to_all | solution.py:102
  58.2 3.2 sort.17
  62.2 537.6 %all-to-all-done = f32[32,6,4,4096]{3,2,1,0:T(4,128)} async-done(((f32[32,6,4,4096]{3,2,1,0:T(4,128)}), f32[32,6,4,4096]{3,2,1,0:T(4,128)}, u32[]{:S(2)}, u32[]{:S(2)}) %all-to-all-start) | async-done | bytes 12582944 | tf_op jit(solution)/shard_map/all_to_all | solution.py:102
  599.8 5.4 gather_fusion
  605.2 0.4 gather.7
  605.6 0.8 fusion.7
  606.4 1.4 fusion.14
  607.8 1.6 fusion.10
  609.5 1.6 fusion.5
  611.1 1.4 fusion.4
  612.6 9.1 %copy.65 = f32[6,4,64,66]{0,1,3,2:T(4,128)} copy(f32[6,4,64,66]{2,3,1,0:T(8,128)S(1)} %pad_maximum_fusion) | data formatting | bytes 811008 | tf_op jit(solution)/shard_map/reshape | solution.py:70
  621.8 12.4 %reshape.116 = f32[16,1,6336]{2,1,0:T(1,128)} reshape(f32[4224,4,6]{2,1,0:T(4,128)} %bitcast.65) | data formatting | bytes 811008
  634.2 9.7 %all-to-all-start.1 = ((f32[16,1,6336]{2,1,0:T(1,128)}), f32[16,1,6336]{2,1,0:T(1,128)S(1)}, u32[]{:S(2)}, u32[]{:S(2)}) async-start(f32[16,1,6336]{2,1,0:T(1,128)} %reshape.116), calls=%async_computation.1 | async-start | bytes 819200 | tf_op jit(solution)/shard_map/all_to_all | solution.py:71
  643.9 0.9 select_select_fusion
  644.8 7.4 %all-to-all-done.1 = f32[16,1,6336]{2,1,0:T(1,128)S(1)} async-done(((f32[16,1,6336]{2,1,0:T(1,128)}), f32[16,1,6336]{2,1,0:T(1,128)S(1)}, u32[]{:S(2)}, u32[]{:S(2)}) %all-to-all-start.1) | async-done | bytes 405536 | tf_op jit(solution)/shard_map/all_to_all | solution.py:71
  652.2 0.5 broadcast.220
  652.7 1.6 reduce.2
  654.3 15.2 %reshape.117 = f32[4224,4,6]{2,1,0:T(4,128)} reshape(f32[16,6336]{1,0:T(8,128)S(1)} %reduce.2) | data formatting | bytes 811008
  669.5 7.6 %copy.51 = f32[6,4,16,264]{3,1,2,0:T(4,128)S(1)} copy(f32[6,4,16,264]{0,1,3,2:T(4,128)} %bitcast.66) | data formatting | bytes 811008 | tf_op jit(solution)/shard_map/all_to_all | solution.py:71
  677.1 0.6 reshape.102
  677.7 0.5 fusion.114
  678.2 0.3 copy.67
  678.5 0.7 fusion.56
  679.5 0.7 fusion.54
  680.2 0.7 fusion.3
  680.9 0.7 fusion.2
  681.6 1.6 convolution_bitcast_fusion
  683.2 36.9 %all-reduce.1 = (f32[6,16]{1,0:T(8,128)S(1)}, f32[16]{0:T(128)S(1)}) all-reduce(f32[6,16]{1,0:T(8,128)S(1)} %convolution_bitcast_fusion, f32[16]{0:T(128)S(1)} %select_reduce_fusion), channel_id=1, replica_groups=mesh['rep'=32,'gz'=16] {'gz'}, use_global_device_ids=true, to_apply=%region_4.5 | all-reduce | flops 112 | bytes 896 | tf_op jit(solution)/shard_map/psum | solution.py:84
  720.1 0.6 broadcast_divide_fusion
  (47 shorter events, 4.3 us)
Async XLA Ops:
  1.9 13.6 %collective-permute-start = (f32[6,1,4096]{2,1,0:T(1,128)S(1)}, f32[6,1,4096]{2,1,0:T(1,128)S(1)}, u32[]{:S(2)}, u32[]{:S(2)}) collective-permute-start(f32[6,1,4096]{2,1,0:T(1,128)S(1)} %get-tuple-element.26), channel_id=1, source_target_pairs={{0,1},{1,2},{2,3},{3,4},{4,5},{5,6},{6,7},{7,8},{8,9},{9,10},{10,1... | collective-permute-start | bytes 294920 | tf_op jit(solution)/shard_map/ppermute | solution.py:19
  3.9 11.7 %collective-permute-start.1 = (f32[6,1,4096]{2,1,0:T(1,128)S(1)}, f32[6,1,4096]{2,1,0:T(1,128)S(1)}, u32[]{:S(2)}, u32[]{:S(2)}) collective-permute-start(f32[6,1,4096]{2,1,0:T(1,128)S(1)} %get-tuple-element.27), channel_id=1, source_target_pairs={{1,0},{2,1},{3,2},{4,3},{5,4},{6,5},{7,6},{8,7},{9,8},{10,9},{11,1... | collective-permute-start | bytes 294920 | tf_op jit(solution)/shard_map/ppermute | solution.py:22
  12.8 1.0 copy-start
  15.2 1.1 copy-start.1
  15.6 0.6 copy-start.4
  15.6 0.7 copy-start.5
  20.3 10.0 %collective-permute-start.2 = (f32[6,1,4096]{2,1,0:T(1,128)}, f32[6,1,4096]{2,1,0:T(1,128)S(1)}, u32[]{:S(2)}, u32[]{:S(2)}) collective-permute-start(f32[6,1,4096]{2,1,0:T(1,128)} %get-tuple-element.20), channel_id=1, source_target_pairs={{0,1},{1,2},{2,3},{3,4},{4,5},{5,6},{6,7},{7,8},{8,9},{9,10},{10,1... | collective-permute-start | bytes 294920 | tf_op jit(solution)/shard_map/ppermute | solution.py:19
  22.2 9.5 %collective-permute-start.3 = (f32[6,1,4096]{2,1,0:T(1,128)S(1)}, f32[6,1,4096]{2,1,0:T(1,128)S(1)}, u32[]{:S(2)}, u32[]{:S(2)}) collective-permute-start(f32[6,1,4096]{2,1,0:T(1,128)S(1)} %get-tuple-element.21), channel_id=1, source_target_pairs={{1,0},{2,1},{3,2},{4,3},{5,4},{6,5},{7,6},{8,7},{9,8},{10,9},{11,1... | collective-permute-start | bytes 294920 | tf_op jit(solution)/shard_map/ppermute | solution.py:22
  30.0 1.7 copy-start.3
  40.1 16.9 %copy-start.2 = (s32[4,64,33]{1,0,2:T(4,128)S(1)}, s32[4,64,33]{1,0,2:T(4,128)}, u32[]{:S(2)}) copy-start(s32[4,64,33]{1,0,2:T(4,128)} %param.11) | copy-start | bytes 101380
  40.1 17.1 %copy-start.6 = (s32[192]{0:T(256)S(1)}, s32[192]{0:T(256)}, u32[]{:S(2)}) copy-start(s32[192]{0:T(256)} %param.9) | copy-start | bytes 2308
  40.1 18.0 %copy-start.7 = (s32[192]{0:T(256)S(1)}, s32[192]{0:T(256)}, u32[]{:S(2)}) copy-start(s32[192]{0:T(256)} %param.10) | copy-start | bytes 2308
  40.1 559.7 %all-to-all-start = ((f32[32,6,4,4096]{3,2,1,0:T(4,128)}), f32[32,6,4,4096]{3,2,1,0:T(4,128)}, u32[]{:S(2)}, u32[]{:S(2)}) async-start(f32[32,6,4,4096]{3,2,1,0:T(4,128)} %stack.2), calls=%async_computation | async-start | bytes 25165824 | tf_op jit(solution)/shard_map/all_to_all | solution.py:102
  634.2 18.0 %all-to-all-start.1 = ((f32[16,1,6336]{2,1,0:T(1,128)}), f32[16,1,6336]{2,1,0:T(1,128)S(1)}, u32[]{:S(2)}, u32[]{:S(2)}) async-start(f32[16,1,6336]{2,1,0:T(1,128)} %reshape.116), calls=%async_computation.1 | async-start | bytes 819200 | tf_op jit(solution)/shard_map/all_to_all | solution.py:71
